TPU v7x, 128 devices: a whole 4x4x4 slice. The times are simulated.
128 devices in a mesh: lev: 4 (over y), col: 32 (over x, z, core).
Axes of the slice: x: 4, y: 4, z: 4, core: 2. Of those that a mesh axis runs over, the one named last changes fastest.
Arguments:
- increment: bfloat16 [3, 128, 131072], P(None, 'lev', 'col'), may hold values from -6 to 6
- jacobian: bfloat16 [1024, 616, 384], P(('lev', 'col')), may hold values from -0.3125 to 0.3125
- departure: bfloat16 [616, 1048576], P(None, ('lev', 'col')), may hold values from -6 to 6
- predictor: float32 [8, 1048576], P(None, ('lev', 'col')), may hold values from -5 to 5
- bias_coef: float32 [616, 8], replicated, may hold values from -1.5 to 1.5
- obs_sigma: float32 [616], replicated, may hold values from 0.5 to 2
- channel_use: int32 [1024, 616], P(('lev', 'col')), may hold values 0 or 1
- send_cols: int32 [128, 128, 8], P(('lev', 'col')), may hold values from 0 to 1023
- obs_slot: int32 [1048576], P(('lev', 'col')), may hold values from 0 to 1023, as said below
Outputs:
- gradient: float32 [3, 128, 131072], P(None, 'lev', 'col')
Inputs may be any that keep to these rules, and one draw needn't show every extreme that they name: obs_slot[j] = s * 8 + k; the slots (s, p, k) named by the observations of device p are, for each s, the first few of the 8, at least 2 of them; some device p names all 8 slots of every device.
All inputs are finite; a program needn't handle non-finite values. No bound on the sum of `channel_use` on one device may be relied on, other than what follows from the above.
Results may differ from a plain program's by a relative error of at most 0.001.
Values may be sent and summed in bfloat16 or wider, within the bound.
A program may use at most 128 MiB of HBM per device.

v0:
```python
import jax
import jax.numpy as jnp
from jax import lax
from jax.sharding import PartitionSpec as P


def fetch_rows(outgoing):
    return lax.all_to_all(outgoing, ("lev", "col"), split_axis=0, concat_axis=0, tiled=True)


def return_rows(outgoing):
    return lax.all_to_all(outgoing, ("lev", "col"), split_axis=0, concat_axis=0, tiled=True)


def observe(profile, jacobian, departure, predictor, bias_coef, obs_sigma, channel_use):
    tile_count = jacobian.shape[0]
    channels = jacobian.shape[1]
    obs_count = profile.shape[0]
    profile_len = profile.shape[1]
    obs_tile = obs_count // tile_count
    tangent = jnp.einsum(
        "tcf,tof->cto",
        jacobian,
        profile.reshape(tile_count, obs_tile, profile_len),
        preferred_element_type=jnp.float32,
    )
    bias_term = jnp.dot(
        bias_coef, predictor, precision=lax.Precision.HIGHEST, preferred_element_type=jnp.float32
    )
    residual = tangent - (departure.astype(jnp.float32) - bias_term).reshape(
        channels, tile_count, obs_tile
    )
    inverse_var = 1.0 / (obs_sigma * obs_sigma)
    scaling = channel_use.astype(jnp.float32).T * inverse_var[:, None]
    forcing = (scaling[:, :, None] * residual).astype(jnp.bfloat16)
    return jnp.einsum(
        "tcf,cto->tof", jacobian, forcing, preferred_element_type=jnp.float32
    ).reshape(obs_count, profile_len)


def on_device(
    increment,
    jacobian,
    departure,
    predictor,
    bias_coef,
    obs_sigma,
    channel_use,
    send_cols,
    obs_slot,
):
    lev_size = lax.axis_size("lev")
    col_size = lax.axis_size("col")
    peer_count = lev_size * col_size
    field_count = increment.shape[0]
    capacity = send_cols.shape[2]
    columns = lax.all_to_all(increment, "lev", split_axis=2, concat_axis=1, tiled=True)
    level_count = columns.shape[1]
    column_count = columns.shape[2]
    profile_len = field_count * level_count
    column_rows = columns.reshape(profile_len, column_count).T
    slot_lists = send_cols[0]
    outgoing = column_rows[slot_lists]
    incoming = fetch_rows(outgoing).reshape(peer_count * capacity, profile_len)
    profile = incoming[obs_slot]
    adjoint = observe(profile, jacobian, departure, predictor, bias_coef, obs_sigma, channel_use)
    slot_adjoint = jax.ops.segment_sum(adjoint, obs_slot, num_segments=peer_count * capacity)
    returned = return_rows(slot_adjoint.reshape(peer_count, capacity, profile_len))
    column_adjoint = jax.ops.segment_sum(
        returned.reshape(peer_count * capacity, profile_len),
        slot_lists.reshape(-1),
        num_segments=column_count,
    )
    field_adjoint = column_adjoint.T.reshape(field_count, level_count, column_count)
    return lax.all_to_all(field_adjoint, "lev", split_axis=1, concat_axis=2, tiled=True)


def solution(mesh):
    return jax.shard_map(
        on_device,
        mesh=mesh,
        in_specs=(
            P(None, "lev", "col"),
            P(("lev", "col"), None, None),
            P(None, ("lev", "col")),
            P(None, ("lev", "col")),
            P(),
            P(),
            P(("lev", "col"), None),
            P(("lev", "col"), None, None),
            P(("lev", "col")),
        ),
        out_specs=P(None, "lev", "col"),
        check_vma=False,
    )
```

profile of v0, /device:TPU:0, one launch (start us, length us, event | category | flops | bytes accessed | tf_op | source)
XLA Modules:
  0.0 255.4 jit_solution(5134098283058532032)
XLA Ops:
  0.0 6.0 %copy.31 = bf16[3,32,4096]{1,0,2:T(4,128)(2,1)} copy(bf16[3,32,4096]{2,1,0:T(8,128)(2,1)} %param.9) | data formatting | bytes 1572864 | tf_op args[0]
  6.0 5.6 %reshape.103 = bf16[4,2,49152]{2,1,0:T(2,128)(2,1)} reshape(bf16[4096,3,32]{2,1,0:T(4,128)(2,1)} %bitcast.49) | data formatting | bytes 1572864
  11.6 4.5 %all-to-all-start = ((bf16[4,2,49152]{2,1,0:T(2,128)(2,1)}), bf16[4,2,49152]{2,1,0:T(2,128)(2,1)S(1)}, u32[]{:S(2)}, u32[]{:S(2)}) async-start(bf16[4,2,49152]{2,1,0:T(2,128)(2,1)} %reshape.103), calls=%async_computation | async-start | bytes 1572864 | tf_op jit(solution)/shard_map/all_to_all | solution.py:57
  16.2 0.1 copy.35
  16.3 0.1 reshape.65
  16.5 12.0 %all-to-all-done = bf16[4,2,49152]{2,1,0:T(2,128)(2,1)S(1)} async-done(((bf16[4,2,49152]{2,1,0:T(2,128)(2,1)}), bf16[4,2,49152]{2,1,0:T(2,128)(2,1)S(1)}, u32[]{:S(2)}, u32[]{:S(2)}) %all-to-all-start) | async-done | bytes 786464 | tf_op jit(solution)/shard_map/all_to_all | solution.py:57
  28.5 4.2 %reshape.104 = bf16[4096,3,32]{2,1,0:T(4,128)(2,1)} reshape(bf16[4,2,49152]{2,1,0:T(2,128)(2,1)S(1)} %all-to-all-done) | data formatting | bytes 1572864
  32.6 5.3 %copy.33 = bf16[3,4,32,1024]{3,2,1,0:T(8,128)(2,1)S(1)} copy(bf16[3,4,32,1024]{2,0,3,1:T(4,128)(2,1)} %bitcast.48) | data formatting | bytes 1572864 | tf_op jit(solution)/shard_map/all_to_all | solution.py:57
  38.0 0.4 copy.34
  38.4 5.0 %gather_fusion = bf16[1024,384]{1,0:T(8,128)(2,1)} fusion(bf16[1024,384]{1,0:T(8,128)(2,1)S(1)} %bitcast.46, s32[1024]{0:T(1024)S(1)} %broadcast_clamp_fusion), kind=kCustom, calls=%fused_computation | custom fusion | bytes 1576960 | tf_op jit(solution)/shard_map/gather | solution.py:63
  43.4 9.2 %all-to-all-start.1 = ((bf16[128,8,384]{2,1,0:T(8,128)(2,1)}), bf16[128,8,384]{2,1,0:T(8,128)(2,1)S(1)}, u32[]{:S(2)}, u32[]{:S(2)}) async-start(bf16[128,8,384]{2,1,0:T(8,128)(2,1)} %bitcast.7), calls=%async_computation.1 | async-start | bytes 1572864 | tf_op jit(solution)/shard_map/all_to_all | solution.py:8
  52.6 20.8 %convert_subtract_fusion = f32[616,8192]{1,0:T(8,128)} fusion(bf16[616,8192]{1,0:T(8,128)(2,1)} %param.11, f32[616,8]{0,1:T(8,128)S(1)} %copy-done.3, f32[8,8192]{1,0:T(8,128)S(1)} %copy-done), kind=kOutput, calls=%fused_computation.7 | convolution fusion | flops 494534656 | bytes 30559488 | tf_op jit(solution)/shard_map/dot_general | solution.py:27
  73.4 33.1 %gather_fusion.1 = bf16[8192,384]{1,0:T(8,128)(2,1)} fusion(bf16[1024,384]{1,0:T(8,128)(2,1)S(1)} %bitcast.45, s32[8192]{0:T(1024)S(1)} %fusion.12), kind=kCustom, calls=%fused_computation.1 | custom fusion | bytes 12615680 | tf_op jit(solution)/shard_map/gather | solution.py:65
  106.5 24.5 %fusion.2 = f32[8,1024,384]{2,1,0:T(8,128)} fusion(bf16[8,616,384]{2,1,0:T(8,128)(2,1)} %param.10, f32[77,8,8,1024]{3,2,1,0:T(8,128)} %bitcast.47, f32[616,8]{0,1:T(8,128)S(1)} %multiply_bitcast_fusion, bf16[8,1024,384]{2,1,0:T(8,128)(2,1)} %bitcast.50), kind=kOutput, calls=%fused_computation.8 | convolution fusion | flops 7766212608 | bytes 42863872 | tf_op jit(solution)/shard_map/tcf,cto->tof/dot_general | solution.py:36
  131.0 50.4 %scatter_custom_fusion = f32[1024,384]{1,0:T(8,128)} fusion(s32[8192]{0:T(1024)S(1)} %copy-done.2, f32[8192,384]{1,0:T(8,128)} %bitcast.55, f32[]{:T(128)} %constant.4.clone.1), kind=kCustom, calls=%fused_computation.14 | custom fusion | flops 3145728 | bytes 1573376 | tf_op jit(solution)/shard_map/scatter-add | solution.py:67
  181.5 9.6 %all-to-all-start.2 = ((f32[128,8,384]{2,1,0:T(8,128)}), f32[128,8,384]{2,1,0:T(8,128)S(1)}, u32[]{:S(2)}, u32[]{:S(2)}) async-start(f32[128,8,384]{2,1,0:T(8,128)} %bitcast.12), calls=%async_computation.2 | async-start | bytes 3145728 | tf_op jit(solution)/shard_map/all_to_all | solution.py:12
  191.0 0.1 copy.30
  191.2 24.7 %all-to-all-done.2 = f32[128,8,384]{2,1,0:T(8,128)S(1)} async-done(((f32[128,8,384]{2,1,0:T(8,128)}), f32[128,8,384]{2,1,0:T(8,128)S(1)}, u32[]{:S(2)}, u32[]{:S(2)}) %all-to-all-start.2) | async-done | bytes 1572896 | tf_op jit(solution)/shard_map/all_to_all | solution.py:12
  215.9 7.1 %scatter_custom_fusion.1 = f32[1024,384]{1,0:T(8,128)S(1)} fusion(s32[1024]{0:T(1024)S(1)} %reshape.89, f32[128,8,384]{2,1,0:T(8,128)S(1)} %all-to-all-done.2, f32[]{:T(128)} %constant.4.clone.1), kind=kCustom, calls=%fused_computation.11 | custom fusion | flops 393216 | bytes 3145732 | tf_op jit(solution)/shard_map/scatter-add | solution.py:69
  223.0 0.5 copy.37
  223.5 1.1 copy.38
  224.6 28.6 %all_to_all.43 = f32[3,128,1024]{2,0,1:T(4,128)S(1)} all-to-all(f32[3,128,1024]{2,0,1:T(4,128)S(1)} %copy.38), channel_id=1, replica_groups=mesh['lev'=4,'col'=32] {'lev'}, dimensions={1} | all-to-all | bytes 3145728 | tf_op jit(solution)/shard_map/all_to_all | solution.py:75
  253.2 0.9 copy.39
  254.1 1.3 copy.44
  (21 shorter events, 0.2 us)
Async XLA Ops:
  0.0 52.6 %copy-start = (f32[8,8192]{1,0:T(8,128)S(1)}, f32[8,8192]{1,0:T(8,128)}, u32[]{:S(2)}) copy-start(f32[8,8192]{1,0:T(8,128)} %param.12) | copy-start | bytes 786436
  6.0 10.1 %copy-start.5 = (s32[1,128,8]{1,2,0:T(8,128)S(1)}, s32[1,128,8]{1,2,0:T(8,128)}, u32[]{:S(2)}) copy-start(s32[1,128,8]{1,2,0:T(8,128)} %param.16) | copy-start | bytes 12292
  6.0 10.4 %copy-start.6 = (f32[616]{0:T(1024)S(1)}, f32[616]{0:T(1024)}, u32[]{:S(2)}) copy-start(f32[616]{0:T(1024)} %param.14) | copy-start | bytes 7396
  6.0 10.4 %copy-start.4 = (s32[8,616]{1,0:T(8,128)S(1)}, s32[8,616]{1,0:T(8,128)}, u32[]{:S(2)}) copy-start(s32[8,616]{1,0:T(8,128)} %param.15) | copy-start | bytes 59140
  6.0 10.4 %copy-start.2 = (s32[8192]{0:T(1024)S(1)}, s32[8192]{0:T(1024)}, u32[]{:S(2)}) copy-start(s32[8192]{0:T(1024)} %param.17) | copy-start | bytes 98308
  11.6 16.8 %all-to-all-start = ((bf16[4,2,49152]{2,1,0:T(2,128)(2,1)}), bf16[4,2,49152]{2,1,0:T(2,128)(2,1)S(1)}, u32[]{:S(2)}, u32[]{:S(2)}) async-start(bf16[4,2,49152]{2,1,0:T(2,128)(2,1)} %reshape.103), calls=%async_computation | async-start | bytes 1572864 | tf_op jit(solution)/shard_map/all_to_all | solution.py:57
  38.3 14.2 %copy-start.3 = (f32[616,8]{0,1:T(8,128)S(1)}, f32[616,8]{0,1:T(8,128)}, u32[]{:S(2)}) copy-start(f32[616,8]{0,1:T(8,128)} %param.13) | copy-start | bytes 59140
  43.4 30.0 %all-to-all-start.1 = ((bf16[128,8,384]{2,1,0:T(8,128)(2,1)}), bf16[128,8,384]{2,1,0:T(8,128)(2,1)S(1)}, u32[]{:S(2)}, u32[]{:S(2)}) async-start(bf16[128,8,384]{2,1,0:T(8,128)(2,1)} %bitcast.7), calls=%async_computation.1 | async-start | bytes 1572864 | tf_op jit(solution)/shard_map/all_to_all | solution.py:8
  181.5 34.5 %all-to-all-start.2 = ((f32[128,8,384]{2,1,0:T(8,128)}), f32[128,8,384]{2,1,0:T(8,128)S(1)}, u32[]{:S(2)}, u32[]{:S(2)}) async-start(f32[128,8,384]{2,1,0:T(8,128)} %bitcast.12), calls=%async_computation.2 | async-start | bytes 3145728 | tf_op jit(solution)/shard_map/all_to_all | solution.py:12
  224.5 30.9 %copy-start.1 = (f32[8,8192]{1,0:T(8,128)S(1)}, f32[8,8192]{1,0:T(8,128)}, u32[]{:S(2)}) copy-start(f32[8,8192]{1,0:T(8,128)} %param.12) | copy-start | bytes 786436
where the time goes:
time: 256 us; the launch traced here: 255 us
  local copies, waits for them, and re-layouts  63.8 us (25%)
  other arithmetic  57.5 us (22%)
  matrix products  45.3 us (18%)
  waiting for transfers between devices  36.7 us (14%)
  blocking collectives  28.6 us (11%)
  starting transfers between devices  23.3 us (9%)
    scatter-add x1, other arithmetic, on_device(): jax.ops.segment_sum(adjoint, obs_slot, num_segments=peer_count * capacity)  50.4 us
    gather x1, local copies, waits for them, and re-layouts, on_device(): profile = incoming[obs_slot]  33.1 us
    all_to_all x1, blocking collectives, on_device(): lax.all_to_all(field_adjoint, 'lev', split_axis=1, concat_axis=2, tiled=T...  28.6 us
    all_to_all x1, waiting for transfers between devices, return_rows(): lax.all_to_all(outgoing, ('lev', 'col'), split_axis=0, concat_axis=0, til...  24.7 us
    dot_general x1, matrix products, observe(): jnp.einsum('tcf,cto->tof', jacobian, forcing, preferred_element_type=jnp....  24.5 us
    dot_general x1, matrix products, observe(): jnp.dot(bias_coef, predictor, precision=lax.Precision.HIGHEST, preferred_...  20.8 us
    unnamed x18, local copies, waits for them, and re-layouts  15.9 us
    all_to_all x1, waiting for transfers between devices, on_device(): lax.all_to_all(increment, 'lev', split_axis=2, concat_axis=1, tiled=True)  12 us
  transfers between devices with their start and end apart: 3, of which 2 were waited for; matrix products, arithmetic and copies ran while one was open for 8% of the time, Pallas kernels for 0%

commit v1 on v0

--- a/solution.py
+++ b/solution.py
@@ -2,6 +2,21 @@
 import jax.numpy as jnp
 from jax import lax
 from jax.sharding import PartitionSpec as P
+from jax.lax import axis_index, axis_size, ppermute
+
+
+def extend_cube(vector, dimension_no, sheet):
+    block_now, p_next = (vector.shape[:dimension_no], vector.shape[dimension_no + 1 :])
+    t_next = vector.reshape(*block_now, sheet, -1, *p_next)
+    return jnp.moveaxis(t_next, dimension_no, 0)
+
+
+def strings_build(xin, dim_no):
+    xin = jnp.moveaxis(xin, 0, dim_no)
+    side_arr = xin.shape
+    return xin.reshape(
+        *side_arr[:dim_no], side_arr[dim_no] * side_arr[dim_no + 1], *side_arr[dim_no + 2 :]
+    )
 
 
 def fetch_rows(outgoing):
@@ -54,7 +69,20 @@
     peer_count = lev_size * col_size
     field_count = increment.shape[0]
     capacity = send_cols.shape[2]
-    columns = lax.all_to_all(increment, "lev", split_axis=2, concat_axis=1, tiled=True)
+    e_now = axis_size("lev")
+    x_now = axis_index("lev")
+    step_out, reply = (e_now, x_now)
+    z_new = extend_cube(increment, 2, step_out)
+    m_next = z_new
+    for dev_i in range(1, step_out):
+        carry_in, tile_out = ((reply + dev_i) % step_out, (reply - dev_i) % step_out)
+        shaped = lax.dynamic_index_in_dim(z_new, carry_in, 0)
+        slots = []
+        for dev_j in range(step_out):
+            slots.append((dev_j, (dev_j + dev_i) % step_out))
+        mat_out = ppermute(shaped, "lev", slots)
+        m_next = lax.dynamic_update_slice_in_dim(m_next, mat_out, tile_out, axis=0)
+    columns = strings_build(m_next, 1)
     level_count = columns.shape[1]
     column_count = columns.shape[2]
     profile_len = field_count * level_count

time: 256 us -> 251 us (0.980)
  local copies, waits for them, and re-layouts: 63.8 us -> 54.4 us
  starting transfers between devices: 23.3 us -> 27 us
    unnamed x18 -> x15, local copies, waits for them, and re-layouts: 15.9 us -> 0.13 us
    ppermute x0 -> x3, waiting for transfers between devices: none -> 13 us  [on_device(): mat_out = ppermute(shaped, 'lev', slots)]
    all_to_all x1 -> x0, waiting for transfers between devices: 12 us -> none  [on_device(): lax.all_to_all(increment, 'lev', split_axis=2, concat_axis=1, tiled=True)]
    dynamic_update_slice x0 -> x3, local copies, waits for them, and re-layouts: none -> 7.9 us  [on_device(): m_next = lax.dynamic_update_slice_in_dim(m_next, mat_out, tile_out, axis=0)]
    ppermute x0 -> x3, starting transfers between devices: none -> 5.98 us  [on_device(): mat_out = ppermute(shaped, 'lev', slots)]
    all_to_all x1 -> x0, local copies, waits for them, and re-layouts: 5.34 us -> none  [on_device(): lax.all_to_all(increment, 'lev', split_axis=2, concat_axis=1, tiled=True)]
    all_to_all x1 -> x0, starting transfers between devices: 4.55 us -> none  [on_device(): lax.all_to_all(increment, 'lev', split_axis=2, concat_axis=1, tiled=True)]
  transfers between devices with their start and end apart: 3 -> 5, of which waited for: 2 -> 3; matrix products, arithmetic and copies ran while one was open for 8% -> 11% of each run, Pallas kernels for 0% -> 0%
where the time goes in v1:
time: 251 us
  other arithmetic  57.5 us (23%)
  local copies, waits for them, and re-layouts  54.4 us (22%)
  matrix products  45.2 us (18%)
  waiting for transfers between devices  37.6 us (15%)
  blocking collectives  28.6 us (11%)
  starting transfers between devices  27 us (11%)
    scatter-add x1, other arithmetic, on_device(): jax.ops.segment_sum(adjoint, obs_slot, num_segments=peer_count * capacity)  50.4 us
    gather x1, local copies, waits for them, and re-layouts, on_device(): profile = incoming[obs_slot]  33.1 us
    all_to_all x1, blocking collectives, on_device(): lax.all_to_all(field_adjoint, 'lev', split_axis=1, concat_axis=2, tiled=T...  28.6 us
    all_to_all x1, waiting for transfers between devices, return_rows(): lax.all_to_all(outgoing, ('lev', 'col'), split_axis=0, concat_axis=0, til...  24.7 us
    dot_general x1, matrix products, observe(): jnp.einsum('tcf,cto->tof', jacobian, forcing, preferred_element_type=jnp....  24.5 us
    dot_general x1, matrix products, observe(): jnp.dot(bias_coef, predictor, precision=lax.Precision.HIGHEST, preferred_...  20.8 us
    ppermute x3, waiting for transfers between devices, on_device(): mat_out = ppermute(shaped, 'lev', slots)  13 us
    all_to_all x1, starting transfers between devices, fetch_rows(): lax.all_to_all(outgoing, ('lev', 'col'), split_axis=0, concat_axis=0, til...  11.5 us
  transfers between devices with their start and end apart: 5, of which 3 were waited for; matrix products, arithmetic and copies ran while one was open for 11% of the time, Pallas kernels for 0%

profile of v1, /device:TPU:0, one launch (start us, length us, event | category | flops | bytes accessed | tf_op | source)
XLA Modules:
  0.0 250.8 jit_solution(10784754709084254040)
XLA Ops:
  0.1 2.3 reshape.57
  2.4 1.2 dynamic-slice_bitcast_fusion
  3.6 1.7 collective-permute-start
  5.4 2.9 %collective-permute-start.1 = (bf16[1,3,32,1024]{3,0,2,1:T(2,128)(2,1)S(1)}, bf16[1,3,32,1024]{3,0,2,1:T(2,128)(2,1)S(1)}, u32[]{:S(2)}, u32[]{:S(2)}) collective-permute-start(bf16[1,3,32,1024]{3,0,2,1:T(2,128)(2,1)S(1)} %get-tuple-element.6), channel_id=1, source_target_pairs={{0,64},{32,96},{64,0},{96,32},{1,65},{33,97},{65,1},{97,33},{2,66}... | collective-permute-start | bytes 589832 | tf_op jit(solution)/shard_map/ppermute | solution.py:83
  8.3 1.3 collective-permute-start.2
  9.9 6.0 %collective-permute-done = bf16[1,3,32,1024]{3,0,2,1:T(2,128)(2,1)S(1)} collective-permute-done((bf16[1,3,32,1024]{3,0,2,1:T(2,128)(2,1)S(1)}, bf16[1,3,32,1024]{3,0,2,1:T(2,128)(2,1)S(1)}, u32[]{:S(2)}, u32[]{:S(2)}) %collective-permute-start) | collective-permute-done | bytes 196640 | tf_op jit(solution)/shard_map/ppermute | solution.py:83
  15.9 2.6 %dynamic_update_slice.9 = bf16[4,3,32,1024]{3,0,2,1:T(4,128)(2,1)S(1)} dynamic-update-slice(bf16[4,3,32,1024]{3,0,2,1:T(4,128)(2,1)S(1)} %bitcast.50, bf16[1,3,32,1024]{3,0,2,1:T(2,128)(2,1)S(1)} %collective-permute-done, s32[]{:T(128)S(6)} %select_n.62, s32[]{:T(128)} %constant.57.clone.1, s32[]{:T(128)} %constant.57.clone.1, s32[]{:T(128)} %constant.57.clone.1) | dynamic-update-slice | bytes 393220 | tf_op jit(solution)/shard_map/dynamic_update_slice | solution.py:84
  18.6 7.0 %collective-permute-done.1 = bf16[1,3,32,1024]{3,0,2,1:T(2,128)(2,1)S(1)} collective-permute-done((bf16[1,3,32,1024]{3,0,2,1:T(2,128)(2,1)S(1)}, bf16[1,3,32,1024]{3,0,2,1:T(2,128)(2,1)S(1)}, u32[]{:S(2)}, u32[]{:S(2)}) %collective-permute-start.1) | collective-permute-done | bytes 196640 | tf_op jit(solution)/shard_map/ppermute | solution.py:83
  25.5 2.6 %dynamic_update_slice.10 = bf16[4,3,32,1024]{3,0,2,1:T(4,128)(2,1)S(1)} dynamic-update-slice(bf16[4,3,32,1024]{3,0,2,1:T(4,128)(2,1)S(1)} %dynamic_update_slice.9, bf16[1,3,32,1024]{3,0,2,1:T(2,128)(2,1)S(1)} %collective-permute-done.1, s32[]{:T(128)S(6)} %select_n.66, s32[]{:T(128)} %constant.57.clone.1, s32[]{:T(128)} %constant.57.clone.1, s32[]{:T(128)} %constant.57.clone.1) | dynamic-update-slice | bytes 393220 | tf_op jit(solution)/shard_map/dynamic_update_slice | solution.py:84
  28.2 2.7 %dynamic_update_slice.11 = bf16[4,3,32,1024]{3,0,2,1:T(4,128)(2,1)S(1)} dynamic-update-slice(bf16[4,3,32,1024]{3,0,2,1:T(4,128)(2,1)S(1)} %dynamic_update_slice.10, bf16[1,3,32,1024]{3,0,2,1:T(2,128)(2,1)S(1)} %collective-permute-done.2, s32[]{:T(128)S(6)} %select_n.70, s32[]{:T(128)} %constant.57.clone.1, s32[]{:T(128)} %constant.57.clone.1, s32[]{:T(128)} %constant.57.clone.1) | dynamic-update-slice | bytes 393220 | tf_op jit(solution)/shard_map/dynamic_update_slice | solution.py:84
  31.5 5.0 %gather_fusion = bf16[1024,384]{1,0:T(8,128)(2,1)} fusion(bf16[1024,384]{1,0:T(8,128)(2,1)S(1)} %bitcast.48, s32[1024]{0:T(1024)S(1)} %broadcast_clamp_fusion), kind=kCustom, calls=%fused_computation | custom fusion | bytes 1576960 | tf_op jit(solution)/shard_map/gather | solution.py:91
  36.5 11.5 %all-to-all-start = ((bf16[128,8,384]{2,1,0:T(8,128)(2,1)}), bf16[128,8,384]{2,1,0:T(8,128)(2,1)S(1)}, u32[]{:S(2)}, u32[]{:S(2)}) async-start(bf16[128,8,384]{2,1,0:T(8,128)(2,1)} %bitcast.9), calls=%async_computation | async-start | bytes 1572864 | tf_op jit(solution)/shard_map/all_to_all | solution.py:23
  47.9 20.8 %convert_subtract_fusion = f32[616,8192]{1,0:T(8,128)} fusion(bf16[616,8192]{1,0:T(8,128)(2,1)} %param.11, f32[616,8]{0,1:T(8,128)S(1)} %copy-done.3, f32[8,8192]{1,0:T(8,128)S(1)} %copy-done), kind=kOutput, calls=%fused_computation.7 | convolution fusion | flops 494534656 | bytes 30559488 | tf_op jit(solution)/shard_map/dot_general | solution.py:42
  68.7 33.1 %gather_fusion.1 = bf16[8192,384]{1,0:T(8,128)(2,1)} fusion(bf16[1024,384]{1,0:T(8,128)(2,1)S(1)} %bitcast.47, s32[8192]{0:T(1024)S(1)} %fusion.12), kind=kCustom, calls=%fused_computation.1 | custom fusion | bytes 12615680 | tf_op jit(solution)/shard_map/gather | solution.py:93
  101.8 24.5 %fusion.2 = f32[8,1024,384]{2,1,0:T(8,128)} fusion(bf16[8,616,384]{2,1,0:T(8,128)(2,1)} %param.10, f32[77,8,8,1024]{3,2,1,0:T(8,128)} %bitcast.49, f32[616,8]{0,1:T(8,128)S(1)} %multiply_bitcast_fusion, bf16[8,1024,384]{2,1,0:T(8,128)(2,1)} %bitcast.52), kind=kOutput, calls=%fused_computation.8 | convolution fusion | flops 7766212608 | bytes 42863872 | tf_op jit(solution)/shard_map/tcf,cto->tof/dot_general | solution.py:51
  126.3 50.4 %scatter_custom_fusion = f32[1024,384]{1,0:T(8,128)} fusion(s32[8192]{0:T(1024)S(1)} %copy-done.2, f32[8192,384]{1,0:T(8,128)} %bitcast.57, f32[]{:T(128)} %constant.55.clone.1), kind=kCustom, calls=%fused_computation.14 | custom fusion | flops 3145728 | bytes 1573376 | tf_op jit(solution)/shard_map/scatter-add | solution.py:95
  176.8 9.6 %all-to-all-start.1 = ((f32[128,8,384]{2,1,0:T(8,128)}), f32[128,8,384]{2,1,0:T(8,128)S(1)}, u32[]{:S(2)}, u32[]{:S(2)}) async-start(f32[128,8,384]{2,1,0:T(8,128)} %bitcast.14), calls=%async_computation.1 | async-start | bytes 3145728 | tf_op jit(solution)/shard_map/all_to_all | solution.py:27
  186.6 24.7 %all-to-all-done.1 = f32[128,8,384]{2,1,0:T(8,128)S(1)} async-done(((f32[128,8,384]{2,1,0:T(8,128)}), f32[128,8,384]{2,1,0:T(8,128)S(1)}, u32[]{:S(2)}, u32[]{:S(2)}) %all-to-all-start.1) | async-done | bytes 1572896 | tf_op jit(solution)/shard_map/all_to_all | solution.py:27
  211.2 7.1 %scatter_custom_fusion.1 = f32[1024,384]{1,0:T(8,128)S(1)} fusion(s32[1024]{0:T(1024)S(1)} %reshape.91, f32[128,8,384]{2,1,0:T(8,128)S(1)} %all-to-all-done.1, f32[]{:T(128)} %constant.55.clone.1), kind=kCustom, calls=%fused_computation.11 | custom fusion | flops 393216 | bytes 3145732 | tf_op jit(solution)/shard_map/scatter-add | solution.py:97
  218.3 0.5 copy.48
  218.8 1.1 copy.49
  219.9 28.6 %all_to_all.28 = f32[3,128,1024]{2,0,1:T(4,128)S(1)} all-to-all(f32[3,128,1024]{2,0,1:T(4,128)S(1)} %copy.49), channel_id=1, replica_groups=mesh['lev'=4,'col'=32] {'lev'}, dimensions={1} | all-to-all | bytes 3145728 | tf_op jit(solution)/shard_map/all_to_all | solution.py:103
  248.5 0.9 copy.50
  249.4 1.3 copy.53
  (27 shorter events, 1.0 us)
Async XLA Ops:
  0.0 47.9 %copy-start = (f32[8,8192]{1,0:T(8,128)S(1)}, f32[8,8192]{1,0:T(8,128)}, u32[]{:S(2)}) copy-start(f32[8,8192]{1,0:T(8,128)} %param.12) | copy-start | bytes 786436
  0.0 9.6 %copy-start.5 = (s32[1,128,8]{1,2,0:T(8,128)S(1)}, s32[1,128,8]{1,2,0:T(8,128)}, u32[]{:S(2)}) copy-start(s32[1,128,8]{1,2,0:T(8,128)} %param.16) | copy-start | bytes 12292
  0.0 9.8 %copy-start.2 = (s32[8192]{0:T(1024)S(1)}, s32[8192]{0:T(1024)}, u32[]{:S(2)}) copy-start(s32[8192]{0:T(1024)} %param.17) | copy-start | bytes 98308
  0.0 9.9 %copy-start.6 = (f32[616]{0:T(1024)S(1)}, f32[616]{0:T(1024)}, u32[]{:S(2)}) copy-start(f32[616]{0:T(1024)} %param.14) | copy-start | bytes 7396
  0.0 9.9 %copy-start.4 = (s32[8,616]{1,0:T(8,128)S(1)}, s32[8,616]{1,0:T(8,128)}, u32[]{:S(2)}) copy-start(s32[8,616]{1,0:T(8,128)} %param.15) | copy-start | bytes 59140
  3.6 12.3 %collective-permute-start = (bf16[1,3,32,1024]{3,0,2,1:T(2,128)(2,1)S(1)}, bf16[1,3,32,1024]{3,0,2,1:T(2,128)(2,1)S(1)}, u32[]{:S(2)}, u32[]{:S(2)}) collective-permute-start(bf16[1,3,32,1024]{3,0,2,1:T(2,128)(2,1)S(1)} %get-tuple-element.7), channel_id=1, source_target_pairs={{0,32},{32,64},{64,96},{96,0},{1,33},{33,65},{65,97},{97,1},{2,34}... | collective-permute-start | bytes 589832 | tf_op jit(solution)/shard_map/ppermute | solution.py:83
  5.4 20.2 %collective-permute-start.1 = (bf16[1,3,32,1024]{3,0,2,1:T(2,128)(2,1)S(1)}, bf16[1,3,32,1024]{3,0,2,1:T(2,128)(2,1)S(1)}, u32[]{:S(2)}, u32[]{:S(2)}) collective-permute-start(bf16[1,3,32,1024]{3,0,2,1:T(2,128)(2,1)S(1)} %get-tuple-element.6), channel_id=1, source_target_pairs={{0,64},{32,96},{64,0},{96,32},{1,65},{33,97},{65,1},{97,33},{2,66}... | collective-permute-start | bytes 589832 | tf_op jit(solution)/shard_map/ppermute | solution.py:83
  8.3 19.9 %collective-permute-start.2 = (bf16[1,3,32,1024]{3,0,2,1:T(2,128)(2,1)S(1)}, bf16[1,3,32,1024]{3,0,2,1:T(2,128)(2,1)S(1)}, u32[]{:S(2)}, u32[]{:S(2)}) collective-permute-start(bf16[1,3,32,1024]{3,0,2,1:T(2,128)(2,1)S(1)} %get-tuple-element.5), channel_id=1, source_target_pairs={{0,96},{32,0},{64,32},{96,64},{1,97},{33,1},{65,33},{97,65},{2,98}... | collective-permute-start | bytes 589832 | tf_op jit(solution)/shard_map/ppermute | solution.py:83
  31.4 16.5 %copy-start.3 = (f32[616,8]{0,1:T(8,128)S(1)}, f32[616,8]{0,1:T(8,128)}, u32[]{:S(2)}) copy-start(f32[616,8]{0,1:T(8,128)} %param.13) | copy-start | bytes 59140
  36.5 32.3 %all-to-all-start = ((bf16[128,8,384]{2,1,0:T(8,128)(2,1)}), bf16[128,8,384]{2,1,0:T(8,128)(2,1)S(1)}, u32[]{:S(2)}, u32[]{:S(2)}) async-start(bf16[128,8,384]{2,1,0:T(8,128)(2,1)} %bitcast.9), calls=%async_computation | async-start | bytes 1572864 | tf_op jit(solution)/shard_map/all_to_all | solution.py:23
  176.8 34.5 %all-to-all-start.1 = ((f32[128,8,384]{2,1,0:T(8,128)}), f32[128,8,384]{2,1,0:T(8,128)S(1)}, u32[]{:S(2)}, u32[]{:S(2)}) async-start(f32[128,8,384]{2,1,0:T(8,128)} %bitcast.14), calls=%async_computation.1 | async-start | bytes 3145728 | tf_op jit(solution)/shard_map/all_to_all | solution.py:27
  219.9 30.9 %copy-start.1 = (f32[8,8192]{1,0:T(8,128)S(1)}, f32[8,8192]{1,0:T(8,128)}, u32[]{:S(2)}) copy-start(f32[8,8192]{1,0:T(8,128)} %param.12) | copy-start | bytes 786436
